TPU v7x, 32 devices: a whole 2x2x4 slice. The times are simulated.
32 devices in a mesh: mp: 2 (over core), heads: 8 (over z, y), tok: 2 (over x).
Axes of the slice: x: 2, y: 2, z: 4, core: 2. Of those that a mesh axis runs over, the one named last changes fastest.
Arguments:
- context: bfloat16 [2, 512, 8192], P('mp', None, 'heads'), may hold values from -6 to 6
- out_weight: bfloat16 [2, 8192, 8192], P('mp', 'heads', 'tok'), may hold values from -0.0625 to 0.0625
- skip_states: bfloat16 [2, 512, 8192], P(None, None, 'tok'), may hold values from -6 to 6
- gram_old: float32 [8192, 8192], P('tok', ('mp', 'heads')), may hold values from -1 to 3
- cross_old: float32 [8192, 8192], P('tok', ('mp', 'heads')), may hold values from -30 to 30
- map_old: float32 [8192, 8192], P('tok', ('mp', 'heads')), may hold values from -0.3 to 0.3
Outputs:
- gram_new: float32 [8192, 8192], P('tok', ('mp', 'heads'))
- cross_new: float32 [8192, 8192], P('tok', ('mp', 'heads'))
- map_new: float32 [8192, 8192], P('tok', ('mp', 'heads'))
- residual_new: float32 [8192, 8192], P('tok', ('mp', 'heads'))
All inputs are finite; a program needn't handle non-finite values.
Results may differ from a plain program's by a relative error of at most 0.03.
Values may be sent and summed in bfloat16 or wider, within the bound.
A program may use at most 256 MiB of HBM per device.

v0:
```python
import jax
import jax.numpy as jnp
from jax import lax
from jax.sharding import PartitionSpec as P

decay_keep = 0.75
ridge_weight = 0.1


def from_root(block, axis, holder):
    block = jnp.where(lax.axis_index(axis) == holder, block, jnp.zeros_like(block))
    return lax.psum(block, axis)


def columns(matrix):
    return lax.all_gather(matrix, "tok", axis=0, tiled=True)


def token_inner(left, right):
    return lax.dot_general(
        left, right, (((0,), (0,)), ((), ())), preferred_element_type=jnp.float32
    )


def per_device(context, out_weight, skip_states, gram_old, cross_old, map_old):
    tokens = context.shape[1]
    width_a = gram_old.shape[0]
    width_c = gram_old.shape[1]
    partial_value = jnp.dot(context[0], out_weight[0], preferred_element_type=jnp.float32)
    model_index = lax.axis_index("mp")
    slot_mask = jnp.arange(2, dtype=jnp.int32) == model_index
    slot_terms = jnp.where(slot_mask[:, None, None], partial_value[None, :, :], 0.0)
    summed = lax.psum(slot_terms.astype(jnp.bfloat16), ("mp", "heads")).astype(jnp.float32)
    states = (summed + skip_states.astype(jnp.float32)).astype(jnp.bfloat16)
    source = states[0]
    target = states[1]
    column = lax.axis_index(("mp", "heads"))
    root_index = column * width_c // width_a
    offset = column * width_c - root_index * width_a
    picked = jnp.stack(
        [
            lax.dynamic_slice_in_dim(source, offset, width_c, 1),
            lax.dynamic_slice_in_dim(target, offset, width_c, 1),
        ]
    )
    fetched = from_root(picked, "tok", root_index)
    new_weight = (1.0 - decay_keep) / tokens
    gram_new = decay_keep * gram_old + new_weight * token_inner(source, fetched[0])
    cross_new = decay_keep * cross_old + new_weight * token_inner(source, fetched[1])
    gram_half = gram_new.astype(jnp.bfloat16)
    map_half = map_old.astype(jnp.bfloat16)
    row_panel = lax.all_gather(gram_half, ("mp", "heads"), axis=1, tiled=True)

    def apply_gram(matrix):
        return jnp.dot(row_panel, columns(matrix), preferred_element_type=jnp.float32)

    residual = cross_new - apply_gram(map_half) - ridge_weight * map_old
    applied = apply_gram(residual.astype(jnp.bfloat16)) + ridge_weight * residual
    totals = lax.psum(
        (jnp.sum(residual * residual), jnp.sum(residual * applied)), ("mp", "heads", "tok")
    )
    step_size = totals[0] / totals[1]
    return (gram_new, cross_new, map_old + step_size * residual, residual - step_size * applied)


def solution(mesh):
    placed = (
        P("mp", None, "heads"),
        P("mp", "heads", "tok"),
        P(None, None, "tok"),
        P("tok", ("mp", "heads")),
        P("tok", ("mp", "heads")),
        P("tok", ("mp", "heads")),
    )
    return jax.shard_map(
        per_device,
        mesh=mesh,
        in_specs=placed,
        out_specs=(
            P("tok", ("mp", "heads")),
            P("tok", ("mp", "heads")),
            P("tok", ("mp", "heads")),
            P("tok", ("mp", "heads")),
        ),
        check_vma=False,
    )
```

profile of v0, /device:TPU:0, one launch (start us, length us, event | category | flops | bytes accessed | tf_op | source)
XLA Modules:
  0.0 940.5 jit_solution(4489660221661309988)
XLA Ops:
  7.2 0.0 copy-start
  7.2 0.0 all-reduce.4.cloned.1.call-start
  7.2 1.2 copy-done
  8.4 8.1 fusion
  16.5 5.4 select_convert_fusion
  21.9 0.0 all-reduce.4.cloned.1.call-update
  21.9 0.0 all-reduce.6.cloned.1.call-start
  22.0 172.7 %all-reduce.4.cloned.1.call-done = bf16[2,512,4096]{2,1,0:T(8,128)(2,1)} async-done(((bf16[2,512,4096]{2,1,0:T(8,128)(2,1)}), bf16[2,512,4096]{2,1,0:T(8,128)(2,1)}) %all-reduce.4.cloned.1.call-update) | async-done | bytes 8388624 | tf_op jit(solution)/shard_map/psum | solution.py:33
  194.7 7.5 add_convert_fusion
  202.2 0.0 copy-start.2
  202.2 1.0 fusion.7
  203.3 2.4 copy-done.2
  205.6 0.1 constant_dynamic-slice_fusion
  205.7 1.1 maximum_select_fusion
  206.8 0.0 all-reduce.6.cloned.1.call-update
  206.8 0.0 all-gather.6.cloned.1.call-start
  206.9 5.9 convert_element_type.26
  212.8 0.0 all-gather.6.cloned.1.call-update
  212.8 0.0 all-gather.4.cloned.1.call-start
  212.9 34.0 %all-reduce.6.cloned.1.call-done = bf16[2,512,512]{2,1,0:T(8,128)(2,1)} async-done(((bf16[2,512,512]{2,1,0:T(8,128)(2,1)}), bf16[2,512,512]{2,1,0:T(8,128)(2,1)}) %all-reduce.6.cloned.1.call-update) | async-done | bytes 1048592 | tf_op jit(solution)/shard_map/psum | solution.py:12
  246.9 0.0 copy-start.3
  246.9 13.9 %fusion.8 = (bf16[4096,512]{1,0:T(8,128)(2,1)}, f32[4096,512]{1,0:T(8,128)}) fusion(bf16[2,512,512]{2,1,0:T(8,128)(2,1)} %all-reduce.6.cloned.1.call-done, bf16[2,512,4096]{2,1,0:T(8,128)(2,1)} %copy-done.2, f32[4096,512]{1,0:T(8,128)} %param.9), kind=kOutput, calls=%fused_computation.24 | convolution fusion | flops 2155872256 | bytes 25690112 | tf_op jit(solution)/shard_map/dot_general | solution.py:20
  260.8 0.0 all-gather.4.cloned.1.call-update
  260.8 0.2 all-gather.8.cloned.1.call-start
  261.0 0.0 copy-done.3
  261.0 11.7 %multiply_add_fusion.2 = f32[4096,512]{1,0:T(8,128)} fusion(f32[4096,512]{1,0:T(8,128)} %param.10, bf16[2,512,512]{2,1,0:T(8,128)(2,1)S(1)} %copy-done.3, bf16[2,512,4096]{2,1,0:T(8,128)(2,1)} %copy-done.2), kind=kOutput, calls=%fused_computation.10 | convolution fusion | flops 2153775104 | bytes 21495808 | tf_op jit(solution)/shard_map/dot_general | solution.py:20
  272.7 79.7 %all-gather.6.cloned.1.call-done = bf16[8192,512]{1,0:T(8,128)(2,1)} async-done(((bf16[4096,512]{1,0:T(8,128)(2,1)}), bf16[8192,512]{1,0:T(8,128)(2,1)}) %all-gather.6.cloned.1.call-update) | async-done | bytes 8388624 | tf_op jit(solution)/shard_map/all_gather | solution.py:16
  352.5 328.2 %all-gather.4.cloned.1.call-done = bf16[4096,8192]{1,0:T(8,128)(2,1)} async-done(((bf16[4096,512]{1,0:T(8,128)(2,1)}), bf16[4096,8192]{1,0:T(8,128)(2,1)}) %all-gather.4.cloned.1.call-update) | async-done | bytes 67108880 | tf_op jit(solution)/shard_map/all_gather | solution.py:52
  680.7 47.0 %fusion.9 = (bf16[4096,512]{1,0:T(8,128)(2,1)}, f32[4096,512]{1,0:T(8,128)}) fusion(f32[4096,512]{1,0:T(8,128)} %param.11, f32[4096,512]{1,0:T(8,128)} %multiply_add_fusion.2, bf16[4096,8192]{1,0:T(8,128)(2,1)} %all-gather.4.cloned.1.call-done, bf16[8192,512]{1,0:T(8,128)(2,1)} %all-gather.6.cloned.1.call-done), kind=kOutput, calls=%fused_computation.25 | convolution fusion | flops 34368126976 | bytes 104857600 | tf_op jit(solution)/shard_map/dot_general | solution.py:55
  727.7 0.0 all-gather.8.cloned.1.call-update
  727.7 104.1 %all-gather.8.cloned.1.call-done = bf16[8192,512]{1,0:T(8,128)(2,1)} async-done(((bf16[4096,512]{1,0:T(8,128)(2,1)}), bf16[8192,512]{1,0:T(8,128)(2,1)}) %all-gather.8.cloned.1.call-update) | async-done | bytes 8388624 | tf_op jit(solution)/shard_map/all_gather | solution.py:16
  831.8 45.8 %multiply_reduce_fusion = (f32[]{:T(128)}, f32[]{:T(128)}, f32[4096,512]{1,0:T(8,128)}) fusion(f32[4096,512]{1,0:T(8,128)} %get-tuple-element.15, bf16[4096,8192]{1,0:T(8,128)(2,1)} %all-gather.4.cloned.1.call-done, bf16[8192,512]{1,0:T(8,128)(2,1)} %all-gather.8.cloned.1.call-done), kind=kOutput, calls=%fused_computation.6 | convolution fusion | flops 34372321280 | bytes 92274696 | tf_op jit(solution)/shard_map/dot_general | solution.py:55
  877.6 39.6 %all-reduce = (f32[]{:T(128)}, f32[]{:T(128)}) all-reduce(f32[]{:T(128)} %get-tuple-element.5, f32[]{:T(128)} %get-tuple-element.4), channel_id=1, replica_groups=mesh['mp'=2,'heads'=8,'tok'=2] {'mp','heads','tok'}, use_global_device_ids=true, to_apply=%region_3.4 | all-reduce | flops 2 | bytes 16 | tf_op jit(solution)/shard_map/psum | solution.py:59
  918.5 0.0 copy-start.1
  918.5 15.5 %multiply_subtract_fusion = (f32[4096,512]{1,0:T(8,128)}, f32[4096,512]{1,0:T(8,128)}) fusion(f32[4096,512]{1,0:T(8,128)} %get-tuple-element.15, f32[4096,512]{1,0:T(8,128)} %get-tuple-element.16, f32[]{:T(128)S(6)} %div.14, f32[4096,512]{1,0:T(8,128)} %param.11), kind=kLoop, calls=%fused_computation.4 | loop fusion | flops 12582912 | bytes 41943044 | tf_op jit(solution)/shard_map/sub | solution.py:63
  934.0 0.0 copy-done.1
  (1 shorter events, 0.0 us)
Async XLA Ops:
  7.2 1.2 copy-start
  7.2 187.5 %all-reduce.4.cloned.1.call-start = ((), (), s32[]{:S(2)}) async-start(), calls=%async_computation | async-start | bytes 16777216 | tf_op jit(solution)/shard_map/psum | solution.py:33
  21.9 224.9 %all-reduce.6.cloned.1.call-start = ((), (), s32[]{:S(2)}) async-start(), calls=%async_computation.1 | async-start | bytes 2097152 | tf_op jit(solution)/shard_map/psum | solution.py:12
  202.2 3.4 copy-start.2
  206.8 145.6 %all-gather.6.cloned.1.call-start = ((), (), s32[]{:S(2)}) async-start(), calls=%async_computation.3 | async-start | bytes 12582912 | tf_op jit(solution)/shard_map/all_gather | solution.py:16
  212.8 467.8 %all-gather.4.cloned.1.call-start = ((), (), s32[]{:S(2)}) async-start(), calls=%async_computation.2 | async-start | bytes 71303168 | tf_op jit(solution)/shard_map/all_gather | solution.py:52
  246.9 14.1 %copy-start.3 = (bf16[2,512,512]{2,1,0:T(8,128)(2,1)S(1)}, bf16[2,512,512]{2,1,0:T(8,128)(2,1)}, u32[]{:S(2)}) copy-start(bf16[2,512,512]{2,1,0:T(8,128)(2,1)} %all-reduce.6.cloned.1.call-done) | copy-start | bytes 3145732
  260.8 571.1 %all-gather.8.cloned.1.call-start = ((), (), s32[]{:S(2)}) async-start(), calls=%async_computation.4 | async-start | bytes 12582912 | tf_op jit(solution)/shard_map/all_gather | solution.py:16
  918.5 15.5 %copy-start.1 = (bf16[1,512,1024]{2,1,0:T(8,128)(2,1)S(1)}, bf16[1,512,1024]{2,1,0:T(8,128)(2,1)}, u32[]{:S(2)}) copy-start(bf16[1,512,1024]{2,1,0:T(8,128)(2,1)} %param.6) | copy-start | bytes 3145732
Sparse Core Ops, SparseCore 0:
  22.1 172.6 all-reduce.3
  207.0 39.8 all-reduce.5
  248.4 103.9 all-gather.5
  354.5 326.1 all-gather.3
  727.8 103.9 all-gather.7
where the time goes:
time: 941 us
  waiting for transfers between devices  719 us (76%)
  matrix products  126 us (13%)
  blocking collectives  39.6 us (4%)
  other arithmetic  35.4 us (4%)
  between operations  15.2 us (2%)
    all_gather x1, waiting for transfers between devices, per_device(): row_panel = lax.all_gather(gram_half, ('mp', 'heads'), axis=1, tiled=True)  328 us
    all_gather x2, waiting for transfers between devices, columns(): return lax.all_gather(matrix, 'tok', axis=0, tiled=True)  184 us
    psum x1, waiting for transfers between devices, per_device(): lax.psum(slot_terms.astype(jnp.bfloat16), ('mp', 'heads'))  173 us
    dot_general x2, matrix products, apply_gram(): jnp.dot(row_panel, columns(matrix), preferred_element_type=jnp.float32)  92.8 us
    psum x1, blocking collectives, per_device(): lax.psum((jnp.sum(residual * residual), jnp.sum(residual * applied)), ('m...  39.6 us
    psum x1, waiting for transfers between devices, from_root(): return lax.psum(block, axis)  34 us
    dot_general x2, matrix products, token_inner(): lax.dot_general(left, right, (((0,), (0,)), ((), ())), preferred_element_...  25.6 us
  transfers between devices with their start and end apart: 5, of which 5 were waited for; matrix products, arithmetic and copies ran while one was open for 3% of the time, Pallas kernels for 0%

commit v1 on v0

--- a/solution.py
+++ b/solution.py
@@ -49,7 +49,15 @@
     cross_new = decay_keep * cross_old + new_weight * token_inner(source, fetched[1])
     gram_half = gram_new.astype(jnp.bfloat16)
     map_half = map_old.astype(jnp.bfloat16)
-    row_panel = lax.all_gather(gram_half, ("mp", "heads"), axis=1, tiled=True)
+    ways, here = (lax.axis_size(("mp", "heads")), lax.axis_index(("mp", "heads")))
+    grown, reach = (gram_half, 1)
+    while reach < ways:
+        theirs = lax.ppermute(grown, ("mp", "heads"), [(d, d ^ reach) for d in range(ways)])
+        mine_first = jnp.concatenate([grown, theirs], axis=1)
+        theirs_first = jnp.concatenate([theirs, grown], axis=1)
+        grown = jnp.where(here & reach == 0, mine_first, theirs_first)
+        reach = 2 * reach
+    row_panel = grown
 
     def apply_gram(matrix):
         return jnp.dot(row_panel, columns(matrix), preferred_element_type=jnp.float32)

time: 941 us -> 1740 us (1.85)
  waiting for transfers between devices: 719 us -> 1350 us
  local copies, waits for them, and re-layouts: 4.66 us -> 68.9 us
  other arithmetic: 35.4 us -> 98.5 us
  matrix products: 126 us -> 160 us
    ppermute x0 -> x4, waiting for transfers between devices: none -> 990 us  [per_device(): lax.ppermute(grown, ('mp', 'heads'), [(d, d ^ reach) for d in range(ways)])]
    all_gather x1 -> x0, waiting for transfers between devices: 328 us -> none  [per_device(): row_panel = lax.all_gather(gram_half, ('mp', 'heads'), axis=1, tiled=True)]
    unnamed x8 -> x15, local copies, waits for them, and re-layouts: 3.53 us -> 67.8 us
    select_n x0 -> x3, other arithmetic: none -> 63.7 us  [per_device(): grown = jnp.where(here & reach == 0, mine_first, theirs_first)]
    dot_general x2, matrix products: 92.8 us -> 129 us  [apply_gram(): jnp.dot(row_panel, columns(matrix), preferred_element_type=jnp.float32)]
    all_gather x2, waiting for transfers between devices: 184 us -> 160 us  [columns(): return lax.all_gather(matrix, 'tok', axis=0, tiled=True)]
  transfers between devices with their start and end apart: 5 -> 8, of which waited for: 5 -> 7; matrix products, arithmetic and copies ran while one was open for 3% -> 4% of each run, Pallas kernels for 0% -> 0%
where the time goes in v1:
time: 1740 us
  waiting for transfers between devices  1350 us (78%)
  matrix products  160 us (9%)
  other arithmetic  98.5 us (6%)
  local copies, waits for them, and re-layouts  68.9 us (4%)
  blocking collectives  39.8 us (2%)
    ppermute x4, waiting for transfers between devices, per_device(): lax.ppermute(grown, ('mp', 'heads'), [(d, d ^ reach) for d in range(ways)])  990 us
    psum x1, waiting for transfers between devices, per_device(): lax.psum(slot_terms.astype(jnp.bfloat16), ('mp', 'heads'))  173 us
    all_gather x2, waiting for transfers between devices, columns(): return lax.all_gather(matrix, 'tok', axis=0, tiled=True)  160 us
    dot_general x2, matrix products, apply_gram(): jnp.dot(row_panel, columns(matrix), preferred_element_type=jnp.float32)  129 us
    unnamed x15, local copies, waits for them, and re-layouts  67.8 us
    select_n x3, other arithmetic, per_device(): grown = jnp.where(here & reach == 0, mine_first, theirs_first)  63.7 us
    psum x1, blocking collectives, per_device(): lax.psum((jnp.sum(residual * residual), jnp.sum(residual * applied)), ('m...  39.8 us
  transfers between devices with their start and end apart: 8, of which 7 were waited for; matrix products, arithmetic and copies ran while one was open for 4% of the time, Pallas kernels for 0%

profile of v1, /device:TPU:0, one launch (start us, length us, event | category | flops | bytes accessed | tf_op | source)
XLA Modules:
  0.0 1742.4 jit_solution(8106735107213129773)
XLA Ops:
  7.2 0.0 copy-start
  7.2 0.0 all-reduce.4.cloned.1.call-start
  7.2 1.2 copy-done
  8.4 8.1 fusion.2
  16.5 5.4 select_convert_fusion
  21.9 0.0 all-reduce.4.cloned.1.call-update
  21.9 0.0 all-reduce.6.cloned.1.call-start
  22.0 172.7 %all-reduce.4.cloned.1.call-done = bf16[2,512,4096]{2,1,0:T(8,128)(2,1)} async-done(((bf16[2,512,4096]{2,1,0:T(8,128)(2,1)}), bf16[2,512,4096]{2,1,0:T(8,128)(2,1)}) %all-reduce.4.cloned.1.call-update) | async-done | bytes 8388624 | tf_op jit(solution)/shard_map/psum | solution.py:33
  194.7 7.5 add_convert_fusion
  202.2 0.0 copy-start.2
  202.2 1.0 fusion.11
  203.3 2.4 copy-done.2
  205.6 0.1 constant_dynamic-slice_fusion
  205.7 1.1 maximum_select_fusion.8
  206.8 0.0 all-reduce.6.cloned.1.call-update
  206.8 0.0 all-gather.3.cloned.1.call-start
  206.9 8.9 copy.10
  215.8 31.0 %all-reduce.6.cloned.1.call-done = bf16[2,512,512]{2,1,0:T(8,128)(2,1)} async-done(((bf16[2,512,512]{2,1,0:T(8,128)(2,1)}), bf16[2,512,512]{2,1,0:T(8,128)(2,1)}) %all-reduce.6.cloned.1.call-update) | async-done | bytes 1048592 | tf_op jit(solution)/shard_map/psum | solution.py:12
  246.9 12.4 fusion.12
  259.3 1.5 collective-permute-start
  260.8 91.2 %collective-permute-done = bf16[4096,512]{0,1:T(8,128)(2,1)} collective-permute-done((bf16[4096,512]{0,1:T(8,128)(2,1)}, bf16[4096,512]{0,1:T(8,128)(2,1)}, u32[]{:S(2)}, u32[]{:S(2)}) %collective-permute-start) | collective-permute-done | bytes 4194336 | tf_op jit(solution)/shard_map/ppermute | solution.py:55
  351.9 11.1 maximum_select_fusion.5
  363.0 1.5 collective-permute-start.1
  364.5 180.2 %collective-permute-done.1 = bf16[4096,1024]{0,1:T(8,128)(2,1)} collective-permute-done((bf16[4096,1024]{0,1:T(8,128)(2,1)}, bf16[4096,1024]{0,1:T(8,128)(2,1)}, u32[]{:S(2)}, u32[]{:S(2)}) %collective-permute-start.1) | collective-permute-done | bytes 8388640 | tf_op jit(solution)/shard_map/ppermute | solution.py:55
  544.6 19.0 %maximum_select_fusion.2 = bf16[4096,2048]{0,1:T(8,128)(2,1)} fusion(bf16[4096,1024]{0,1:T(8,128)(2,1)} %collective-permute-done.1, bf16[4096,1024]{0,1:T(8,128)(2,1)} %maximum_select_fusion.5, pred[]{:T(512)S(6)} %eq.30), kind=kLoop, calls=%fused_computation.2 | loop fusion | flops 75497472 | bytes 33554432 | tf_op jit(solution)/shard_map/jit(_where)/select_n | solution.py:58
  563.6 2.4 collective-permute-start.2
  566.0 718.5 %collective-permute-done.2 = bf16[4096,2048]{0,1:T(8,128)(2,1)} collective-permute-done((bf16[4096,2048]{0,1:T(8,128)(2,1)}, bf16[4096,2048]{0,1:T(8,128)(2,1)}, u32[]{:S(2)}, u32[]{:S(2)}) %collective-permute-start.2) | collective-permute-done | bytes 16777248 | tf_op jit(solution)/shard_map/ppermute | solution.py:55
  1284.5 33.6 %maximum_select_fusion.1 = bf16[4096,4096]{0,1:T(8,128)(2,1)} fusion(bf16[4096,2048]{0,1:T(8,128)(2,1)} %collective-permute-done.2, bf16[4096,2048]{0,1:T(8,128)(2,1)} %maximum_select_fusion.2, pred[]{:T(512)S(6)} %eq.29), kind=kLoop, calls=%fused_computation.1 | loop fusion | flops 150994944 | bytes 67108864 | tf_op jit(solution)/shard_map/jit(_where)/select_n | solution.py:58
  1318.2 0.1 collective-permute-start.3
  1318.2 5.9 convert_element_type.26
  1324.2 0.0 all-gather.3.cloned.1.call-update
  1324.2 0.2 all-gather.5.cloned.1.call-start
  1324.4 9.1 copy.16
  1333.5 0.0 copy-start.3
  1333.5 9.5 copy.11
  1343.1 0.0 copy-done.3
  1343.1 10.8 multiply_add_fusion.2
  1353.8 74.7 %all-gather.3.cloned.1.call-done = bf16[8192,512]{1,0:T(8,128)(2,1)} async-done(((bf16[4096,512]{1,0:T(8,128)(2,1)}), bf16[8192,512]{1,0:T(8,128)(2,1)}) %all-gather.3.cloned.1.call-update) | async-done | bytes 8388624 | tf_op jit(solution)/shard_map/all_gather | solution.py:16
  1428.5 0.0 collective-permute-done.3
  1428.5 67.0 %fusion.13 = (bf16[4096,512]{0,1:T(8,128)(2,1)}, f32[4096,512]{0,1:T(8,128)}) fusion(f32[4096,512]{0,1:T(8,128)} %copy.16, f32[4096,512]{0,1:T(8,128)} %multiply_add_fusion.2, bf16[8192,512]{1,0:T(8,128)(2,1)} %all-gather.3.cloned.1.call-done, bf16[4096,4096]{0,1:T(8,128)(2,1)} %collective-permute-done.3, bf16[4096,4096]{0,1:T(8,128)(2,1)} %maximum_select_fusion.1, ...), kind=kOutput, calls=%fused_computation.33 | convolution fusion | flops 34670116864 | bytes 104857600 | tf_op jit(solution)/shard_map/dot_general | solution.py:63
  1495.4 0.0 all-gather.5.cloned.1.call-update
  1495.5 9.2 copy.18
  1504.6 9.5 copy.17
  1514.2 85.5 %all-gather.5.cloned.1.call-done = bf16[8192,512]{0,1:T(8,128)(2,1)} async-done(((bf16[4096,512]{0,1:T(8,128)(2,1)}), bf16[8192,512]{0,1:T(8,128)(2,1)}) %all-gather.5.cloned.1.call-update) | async-done | bytes 8388624 | tf_op jit(solution)/shard_map/all_gather | solution.py:16
  1599.6 62.2 %multiply_reduce_fusion = (f32[]{:T(128)}, f32[]{:T(128)}, f32[4096,512]{0,1:T(8,128)}) fusion(f32[4096,512]{0,1:T(8,128)} %get-tuple-element.19, bf16[8192,512]{0,1:T(8,128)(2,1)} %all-gather.5.cloned.1.call-done, bf16[4096,4096]{0,1:T(8,128)(2,1)} %collective-permute-done.3, bf16[4096,4096]{0,1:T(8,128)(2,1)} %maximum_select_fusion.1, pred[]{:T(512)S(6)} %eq.28), kind=kOutput, calls=%fused_computation.12 | convolution fusion | flops 34674311168 | bytes 92274696 | tf_op jit(solution)/shard_map/dot_general | solution.py:63
  1661.9 39.8 %all-reduce = (f32[]{:T(128)}, f32[]{:T(128)}) all-reduce(f32[]{:T(128)} %get-tuple-element.9, f32[]{:T(128)} %get-tuple-element.8), channel_id=1, replica_groups=mesh['mp'=2,'heads'=8,'tok'=2] {'mp','heads','tok'}, use_global_device_ids=true, to_apply=%region_3.4 | all-reduce | flops 2 | bytes 16 | tf_op jit(solution)/shard_map/psum | solution.py:67
  1703.0 14.9 multiply_subtract_fusion
  1717.9 8.9 copy.20
  1726.9 0.0 copy-start.1
  1726.9 9.0 copy.19
  1735.9 0.0 copy-done.1
  (1 shorter events, 0.0 us)
Async XLA Ops:
  7.2 1.2 copy-start
  7.2 187.5 %all-reduce.4.cloned.1.call-start = ((), (), s32[]{:S(2)}) async-start(), calls=%async_computation | async-start | bytes 16777216 | tf_op jit(solution)/shard_map/psum | solution.py:33
  21.9 224.9 %all-reduce.6.cloned.1.call-start = ((), (), s32[]{:S(2)}) async-start(), calls=%async_computation.1 | async-start | bytes 2097152 | tf_op jit(solution)/shard_map/psum | solution.py:12
  202.2 3.4 copy-start.2
  206.8 1221.6 %all-gather.3.cloned.1.call-start = ((), (), s32[]{:S(2)}) async-start(), calls=%async_computation.2 | async-start | bytes 12582912 | tf_op jit(solution)/shard_map/all_gather | solution.py:16
  259.3 92.6 %collective-permute-start = (bf16[4096,512]{0,1:T(8,128)(2,1)}, bf16[4096,512]{0,1:T(8,128)(2,1)}, u32[]{:S(2)}, u32[]{:S(2)}) collective-permute-start(bf16[4096,512]{0,1:T(8,128)(2,1)} %get-tuple-element.16), channel_id=1, source_target_pairs={{0,2},{2,0},{4,6},{6,4},{8,10},{10,8},{12,14},{14,12},{16,18},{18,... | collective-permute-start | bytes 12582920 | tf_op jit(solution)/shard_map/ppermute | solution.py:55
  363.0 181.6 %collective-permute-start.1 = (bf16[4096,1024]{0,1:T(8,128)(2,1)}, bf16[4096,1024]{0,1:T(8,128)(2,1)}, u32[]{:S(2)}, u32[]{:S(2)}) collective-permute-start(bf16[4096,1024]{0,1:T(8,128)(2,1)} %maximum_select_fusion.5), channel_id=1, source_target_pairs={{0,4},{2,6},{4,0},{6,2},{8,12},{10,14},{12,8},{14,10},{16,20},{18,... | collective-permute-start | bytes 25165832 | tf_op jit(solution)/shard_map/ppermute | solution.py:55
  563.6 720.9 %collective-permute-start.2 = (bf16[4096,2048]{0,1:T(8,128)(2,1)}, bf16[4096,2048]{0,1:T(8,128)(2,1)}, u32[]{:S(2)}, u32[]{:S(2)}) collective-permute-start(bf16[4096,2048]{0,1:T(8,128)(2,1)} %maximum_select_fusion.2), channel_id=1, source_target_pairs={{0,8},{2,10},{4,12},{6,14},{8,0},{10,2},{12,4},{14,6},{16,24},{18,... | collective-permute-start | bytes 50331656 | tf_op jit(solution)/shard_map/ppermute | solution.py:55
  1318.2 110.3 %collective-permute-start.3 = (bf16[4096,4096]{0,1:T(8,128)(2,1)}, bf16[4096,4096]{0,1:T(8,128)(2,1)}, u32[]{:S(2)}, u32[]{:S(2)}) collective-permute-start(bf16[4096,4096]{0,1:T(8,128)(2,1)} %maximum_select_fusion.1), channel_id=1, source_target_pairs={{0,16},{2,18},{4,20},{6,22},{8,24},{10,26},{12,28},{14,30},{16,0},... | collective-permute-start | bytes 100663304 | tf_op jit(solution)/shard_map/ppermute | solution.py:55
  1324.2 275.4 %all-gather.5.cloned.1.call-start = ((), (), s32[]{:S(2)}) async-start(), calls=%async_computation.3 | async-start | bytes 12582912 | tf_op jit(solution)/shard_map/all_gather | solution.py:16
  1333.5 9.5 copy-start.3
  1726.9 9.0 copy-start.1
Sparse Core Ops, SparseCore 0:
  22.1 172.6 all-reduce.3
  207.0 39.8 all-reduce.5
  1324.3 104.1 all-gather.2
  1495.6 103.9 all-gather.4
